TPU v7x, 128 devices: a whole 4x4x4 slice. The times are simulated.
128 devices in a mesh: sub: 32 (over y, x, core), grp: 4 (over z).
Axes of the slice: x: 4, y: 4, z: 4, core: 2. Of those that a mesh axis runs over, the one named last changes fastest.
Arguments:
- right_side: float32 [4096, 256, 128], P(('sub', 'grp')), may hold values from -13 to 13
- diag_blocks: float32 [4096, 128, 128], P(('sub', 'grp')), may hold values from -1 to 5.5, as said below
- couplings: float32 [4096, 4, 128, 128], P(('sub', 'grp')), may hold values from -0.25 to 0.25
- factors: float32 [4096, 128, 128], P(('sub', 'grp')), may hold values from -1 to 1, as said below
- prolong: float32 [4096, 8, 128], P(('sub', 'grp')), may hold values from -1.5 to 1.5
- coarse_inverse: float32 [32, 1024, 1024], P('sub', 'grp'), may hold values from -1 to 1, as said below
- intersection_send: int32 [512], P(('sub', 'grp')), may hold values from 0 to 31, as said below
- neighbours: int32 [4096, 4], P(('sub', 'grp')), may hold values from 0 to 39, as said below
- coarse_pick: int32 [4096], P(('sub', 'grp')), may hold values from 0 to 31, as said below
Outputs:
- solution: float32 [4096, 256, 128], P(('sub', 'grp'))
- residual: float32 [4096, 256, 128], P(('sub', 'grp'))
Inputs may be any that keep to these rules, and one draw needn't show every extreme that they name: `neighbours`: block rows of one device name entries of that device's ext: its 32 own blocks first, then the 4 received from the lower neighbour, then the 4 from the upper one; on every device each of the 8 received blocks is named by some entry. `intersection_send`: each device's 4 entries are distinct local block numbers. `coarse_pick`: each device's 32 entries form a permutation of its local block numbers. `diag_blocks`: diagonal entries lie in 3.5 to 5.5; each off-diagonal entry is at most 1.8 / 128**0.5 in magnitude. `factors`: diagonal entries lie in 0.45 to 0.75; each off-diagonal entry is at most 0.3 / 128**0.5 in magnitude. `coarse_inverse`: diagonal entries lie in 0.3 to 0.6; each off-diagonal entry is at most 0.3 / 1024**0.5 in magnitude.
All inputs are finite; a program needn't handle non-finite values.
Results may differ from a plain program's by a relative error of at most 0.00026.
Values sent between devices are 32-bit elements; how exact they have to be, the bound alone decides.
No kernel may reach another device: no remote copies, remote signals or barrier semaphores. Data moves between devices by JAX's collectives and lax.ppermute only.
A program may use at most 192 MiB of HBM per device.

v0:
```python
import jax
import jax.numpy as jnp
from jax import lax
from jax.sharding import PartitionSpec as P

ITERS = 3


HI = lax.Precision.HIGHEST


def padded_2(cells, sides, width):
    for axis, dim in sides:
        count = lax.axis_size(axis)
        head = lax.slice_in_dim(cells, 0, width, axis=dim)
        tail = lax.slice_in_dim(cells, cells.shape[dim] - width, cells.shape[dim], axis=dim)
        cells = jnp.concatenate(
            [
                lax.ppermute(tail, axis, [(i, (i + 1) % count) for i in range(count)]),
                cells,
                lax.ppermute(head, axis, [((i + 1) % count, i) for i in range(count)]),
            ],
            axis=dim,
        )
    return cells


def fine_part(residual, factors):
    inner = jnp.einsum("nrb,nbc->nrc", residual, factors, precision=HI)
    return jnp.einsum("nrc,nbc->nrb", inner, factors, precision=HI)


def coarse_solve(residual, prolong, coarse_pick, coarse_inverse):
    blocks = residual.shape[0]
    nrhs = residual.shape[1]
    ncoarse = prolong.shape[1]
    groups = lax.axis_size("sub")
    per = blocks // groups
    inverse_rows = coarse_inverse[0]
    coarse_rhs = jnp.einsum("ncb,nrb->ncr", prolong, residual, precision=HI)
    slots = jnp.take(coarse_rhs, coarse_pick, axis=0)
    parcel = slots.reshape(groups, per, ncoarse, nrhs)
    arrived = lax.all_to_all(parcel, "sub", split_axis=0, concat_axis=0, tiled=True)
    span = groups * per * ncoarse
    piece = lax.all_gather(arrived[None], "grp", axis=0, tiled=True)
    flat = piece.reshape(piece.shape[0] * span, nrhs)
    solved = jnp.dot(inverse_rows, flat, precision=HI, preferred_element_type=jnp.float32)
    returned = lax.all_to_all(
        solved.reshape(groups, per, ncoarse, nrhs), "sub", split_axis=0, concat_axis=0, tiled=True
    )
    returned = returned.reshape(blocks, ncoarse, nrhs)
    inverse = jnp.argsort(coarse_pick)
    return jnp.take(returned, inverse, axis=0)


def local(
    right_side,
    diag_blocks,
    couplings,
    factors,
    prolong,
    coarse_inverse,
    intersection_send,
    neighbours,
    coarse_pick,
):
    depth = intersection_send.shape[0]
    solution = jnp.zeros_like(right_side)
    residual = right_side
    for step in range(ITERS):
        fine = fine_part(residual, factors)
        coarse_sol = coarse_solve(residual, prolong, coarse_pick, coarse_inverse)
        coarse = jnp.einsum("ncb,ncr->nrb", prolong, coarse_sol, precision=HI)
        direction = fine + coarse
        padded = padded_2(jnp.take(direction, intersection_send, axis=0), (("sub", 0),), depth)
        extended = jnp.concatenate([direction, padded[:depth], padded[2 * depth :]], axis=0)
        picked = jnp.take(extended, neighbours, axis=0)
        image = jnp.einsum("nrc,nbc->nrb", direction, diag_blocks, precision=HI)
        image = image + jnp.einsum("nkrc,nkbc->nrb", picked, couplings, precision=HI)
        upper_sum, lower_sum = lax.psum(
            (jnp.sum(image * residual), jnp.sum(image * image)), ("sub", "grp")
        )
        alpha = upper_sum / lower_sum
        solution = solution + alpha * direction
        residual = residual - alpha * image
    return (solution, residual)


def solution(mesh):
    return jax.shard_map(
        local,
        mesh=mesh,
        in_specs=(
            P(("sub", "grp"), None, None),
            P(("sub", "grp"), None, None),
            P(("sub", "grp"), None, None, None),
            P(("sub", "grp"), None, None),
            P(("sub", "grp"), None, None),
            P("sub", "grp", None),
            P(("sub", "grp")),
            P(("sub", "grp"), None),
            P(("sub", "grp")),
        ),
        out_specs=(P(("sub", "grp"), None, None), P(("sub", "grp"), None, None)),
        check_vma=False,
    )
```

profile of v0, /device:TPU:1, one launch (start us, length us, event | category | flops | bytes accessed | tf_op | source)
XLA Modules:
  0.0 646.5 jit_solution(3766486168722661375)
XLA Ops:
  7.2 0.8 compare_select_fusion.3
  8.7 5.7 fusion.41
  15.0 0.8 select_bitcast_fusion.2
  15.9 8.6 %all-to-all-start = ((f32[32,1,8,256]{3,2,1,0:T(8,128)}), f32[32,1,8,256]{3,2,1,0:T(8,128)S(1)}, u32[]{:S(2)}, u32[]{:S(2)}) async-start(f32[32,1,8,256]{3,2,1,0:T(8,128)} %select_bitcast_fusion.2), calls=%async_computation | async-start | bytes 524288 | tf_op jit(solution)/shard_map/all_to_all | solution.py:43
  24.5 1.6 sort.21
  26.7 6.7 %all-to-all-done = f32[32,1,8,256]{3,2,1,0:T(8,128)S(1)} async-done(((f32[32,1,8,256]{3,2,1,0:T(8,128)}), f32[32,1,8,256]{3,2,1,0:T(8,128)S(1)}, u32[]{:S(2)}, u32[]{:S(2)}) %all-to-all-start) | async-done | bytes 262176 | tf_op jit(solution)/shard_map/all_to_all | solution.py:43
  35.8 5.6 fusion.39
  41.5 5.3 fusion.40
  46.8 9.1 %all-gather.7.cloned.1.call-done = f32[128,1,8,256]{3,2,1,0:T(8,128)} async-done(((f32[32,1,8,256]{3,2,1,0:T(8,128)}), f32[128,1,8,256]{3,2,1,0:T(8,128)}) %all-gather.7.cloned.1.call-update) | async-done | bytes 1048592 | tf_op jit(solution)/shard_map/all_gather | solution.py:45
  55.9 3.0 convolution_bitcast_fusion.4
  58.9 8.4 %all-to-all-start.1 = ((f32[32,1,8,256]{3,2,1,0:T(8,128)}), f32[32,1,8,256]{3,2,1,0:T(8,128)S(1)}, u32[]{:S(2)}, u32[]{:S(2)}) async-start(f32[32,1,8,256]{3,2,1,0:T(8,128)} %convolution_bitcast_fusion.4), calls=%async_computation.1 | async-start | bytes 524288 | tf_op jit(solution)/shard_map/all_to_all | solution.py:48
  68.2 0.8 copy.26
  70.3 5.9 all-to-all-done.1
  76.9 1.6 gather_fusion.1
  78.6 10.6 %convolution_add_fusion.2 = f32[32,256,128]{2,1,0:T(8,128)} fusion(f32[32,256,128]{2,1,0:T(8,128)} %fusion.40, f32[32,8,128]{2,1,0:T(8,128)S(1)} %copy-done.9, f32[32,8,256]{2,1,0:T(8,128)S(1)} %gather_fusion.1, pred[32]{0:T(512)(128)(4,1)} %compare_and_fusion.2), kind=kOutput, calls=%fused_computation.42 | convolution fusion | flops 101777408 | bytes 8781856 | tf_op jit(solution)/shard_map/ncb,ncr->nrb/dot_general | solution.py:73
  89.2 3.7 gather_fusion.2
  92.9 2.0 broadcast_select_fusion.2
  95.5 12.6 %fusion.42 = f32[32,256,128]{2,1,0:T(8,128)} fusion(f32[32,256,128]{2,1,0:T(8,128)} %convolution_add_fusion.2, f32[32,128,128]{2,1,0:T(8,128)} %param.16), kind=kOutput, calls=%fused_computation.90 | convolution fusion | flops 1610612736 | bytes 10485760 | tf_op jit(solution)/shard_map/nrc,nbc->nrb/dot_general | solution.py:78
  108.1 3.9 pad_maximum_fusion
  112.1 12.4 %gather_fusion.3 = f32[128,256,128]{2,1,0:T(8,128)} fusion(f32[40,256,128]{2,1,0:T(8,128)} %pad_maximum_fusion, s32[1024]{0:T(1024)S(1)} %pad_clamp_fusion), kind=kCustom, calls=%fused_computation.2.clone | custom fusion | bytes 33554944 | tf_op jit(solution)/shard_map/jit(_take)/gather | solution.py:77
  124.4 23.1 %multiply_reduce_fusion.4 = (f32[]{:T(128)}, f32[]{:T(128)}, f32[32,256,128]{2,1,0:T(8,128)}) fusion(f32[32,256,128]{2,1,0:T(8,128)} %param.15, f32[32,256,128]{2,1,0:T(8,128)} %fusion.42, f32[32,4,128,128]{3,2,1,0:T(8,128)} %param.17, f32[32,4,256,128]{3,2,1,0:T(8,128)} %bitcast.96, pred[32,4]{1,0:T(8,128)(4,1)S(1)} %copy.25), kind=kOutput, calls=%fused_computation.38 | convolution fusion | flops 6451888128 | bytes 37748872 | tf_op jit(solution)/shard_map/nkrc,nkbc->nrb/dot_general | solution.py:79
  147.6 76.7 %all-reduce.2 = (f32[]{:T(128)}, f32[]{:T(128)}) all-reduce(f32[]{:T(128)} %get-tuple-element.12, f32[]{:T(128)} %get-tuple-element.11), channel_id=1, replica_groups=mesh['sub'=32,'grp'=4] {'sub','grp'}, use_global_device_ids=true, to_apply=%region_2.6 | all-reduce | flops 2 | bytes 16 | tf_op jit(solution)/shard_map/psum | solution.py:80
  225.6 4.1 multiply_subtract_fusion.2
  229.6 2.0 copy-done.3
  231.6 3.6 convolution_bitcast_fusion.1
  235.3 1.4 gather_fusion.4
  236.7 1.0 select_bitcast_fusion.1
  237.7 13.6 %all_to_all.30 = f32[32,1,8,256]{3,2,1,0:T(8,128)} all-to-all(f32[32,1,8,256]{3,2,1,0:T(8,128)S(1)} %select_bitcast_fusion.1), channel_id=1, replica_groups=mesh['sub'=32,'grp'=4] {'sub'}, dimensions={0} | all-to-all | bytes 524288 | tf_op jit(solution)/shard_map/all_to_all | solution.py:43
  251.3 6.8 %fusion.43 = f32[32,256,128]{2,1,0:T(8,128)} fusion(f32[32,256,128]{2,1,0:T(8,128)} %copy-done.3, f32[32,128,128]{2,1,0:T(8,128)S(1)} %copy-done), kind=kOutput, calls=%fused_computation.91 | convolution fusion | flops 1610612736 | bytes 10485760 | tf_op jit(solution)/shard_map/nrb,nbc->nrc/dot_general | solution.py:29
  258.2 13.2 %all-gather.9.cloned.1.call-done = f32[128,1,8,256]{3,2,1,0:T(8,128)} async-done(((f32[32,1,8,256]{3,2,1,0:T(8,128)}), f32[128,1,8,256]{3,2,1,0:T(8,128)}) %all-gather.9.cloned.1.call-update) | async-done | bytes 1048592 | tf_op jit(solution)/shard_map/all_gather | solution.py:45
  271.3 3.0 convolution_bitcast_fusion.3
  274.3 8.4 %all-to-all-start.3 = ((f32[32,1,8,256]{3,2,1,0:T(8,128)}), f32[32,1,8,256]{3,2,1,0:T(8,128)S(1)}, u32[]{:S(2)}, u32[]{:S(2)}) async-start(f32[32,1,8,256]{3,2,1,0:T(8,128)} %convolution_bitcast_fusion.3), calls=%async_computation.3 | async-start | bytes 524288 | tf_op jit(solution)/shard_map/all_to_all | solution.py:48
  282.8 6.9 %fusion.44 = f32[32,256,128]{2,1,0:T(8,128)} fusion(f32[32,256,128]{2,1,0:T(8,128)} %fusion.43, f32[32,128,128]{2,1,0:T(8,128)S(1)} %copy-done), kind=kOutput, calls=%fused_computation.92 | convolution fusion | flops 1610612736 | bytes 10485760 | tf_op jit(solution)/shard_map/nrc,nbc->nrb/dot_general | solution.py:30
  289.8 1.9 all-to-all-done.3
  292.4 1.6 gather_fusion.5
  294.0 10.7 %convolution_add_fusion.1 = f32[32,256,128]{2,1,0:T(8,128)} fusion(f32[32,256,128]{2,1,0:T(8,128)} %fusion.44, f32[32,8,128]{2,1,0:T(8,128)S(1)} %copy-done.9, f32[32,8,256]{2,1,0:T(8,128)S(1)} %gather_fusion.5, pred[32]{0:T(512)(128)(4,1)S(1)} %copy-done.15), kind=kOutput, calls=%fused_computation.41 | convolution fusion | flops 101777408 | bytes 8781856 | tf_op jit(solution)/shard_map/ncb,ncr->nrb/dot_general | solution.py:73
  304.7 3.7 gather_fusion.6
  308.4 1.1 broadcast_select_fusion.1
  310.5 12.8 %fusion.45 = f32[32,256,128]{2,1,0:T(8,128)} fusion(f32[32,256,128]{2,1,0:T(8,128)} %convolution_add_fusion.1, f32[32,128,128]{2,1,0:T(8,128)} %param.16), kind=kOutput, calls=%fused_computation.93 | convolution fusion | flops 1610612736 | bytes 10485760 | tf_op jit(solution)/shard_map/nrc,nbc->nrb/dot_general | solution.py:78
  323.3 2.7 pad_maximum_fusion.1
  326.0 12.4 %gather_fusion.7 = f32[128,256,128]{2,1,0:T(8,128)} fusion(f32[40,256,128]{2,1,0:T(8,128)} %pad_maximum_fusion.1, s32[1024]{0:T(1024)S(1)} %pad_clamp_fusion), kind=kCustom, calls=%fused_computation.10.clone | custom fusion | bytes 33554944 | tf_op jit(solution)/shard_map/jit(_take)/gather | solution.py:77
  338.4 23.2 %multiply_reduce_fusion.2 = (f32[]{:T(128)}, f32[]{:T(128)}, f32[32,256,128]{2,1,0:T(8,128)}) fusion(f32[32,256,128]{2,1,0:T(8,128)} %copy-done.3, f32[32,256,128]{2,1,0:T(8,128)} %fusion.45, f32[32,4,128,128]{3,2,1,0:T(8,128)} %param.17, f32[32,4,256,128]{3,2,1,0:T(8,128)} %bitcast.97, pred[32,4]{1,0:T(8,128)(4,1)S(1)} %copy.25), kind=kOutput, calls=%fused_computation.35 | convolution fusion | flops 6451888128 | bytes 37748872 | tf_op jit(solution)/shard_map/nkrc,nkbc->nrb/dot_general | solution.py:79
  361.5 66.1 %all-reduce.1 = (f32[]{:T(128)}, f32[]{:T(128)}) all-reduce(f32[]{:T(128)} %get-tuple-element.10, f32[]{:T(128)} %get-tuple-element.9), channel_id=1, replica_groups=mesh['sub'=32,'grp'=4] {'sub','grp'}, use_global_device_ids=true, to_apply=%region_6.10 | all-reduce | flops 2 | bytes 16 | tf_op jit(solution)/shard_map/psum | solution.py:80
  428.9 4.1 multiply_subtract_fusion.1
  433.0 2.0 copy-done.1
  435.0 3.6 convolution_bitcast_fusion
  438.6 1.4 gather_fusion.8
  440.0 1.0 select_bitcast_fusion
  441.1 13.6 %all_to_all.31 = f32[32,1,8,256]{3,2,1,0:T(8,128)} all-to-all(f32[32,1,8,256]{3,2,1,0:T(8,128)S(1)} %select_bitcast_fusion), channel_id=1, replica_groups=mesh['sub'=32,'grp'=4] {'sub'}, dimensions={0} | all-to-all | bytes 524288 | tf_op jit(solution)/shard_map/all_to_all | solution.py:43
  454.7 6.8 %fusion.46 = f32[32,256,128]{2,1,0:T(8,128)} fusion(f32[32,256,128]{2,1,0:T(8,128)} %copy-done.1, f32[32,128,128]{2,1,0:T(8,128)S(1)} %copy-done), kind=kOutput, calls=%fused_computation.94 | convolution fusion | flops 1610612736 | bytes 10485760 | tf_op jit(solution)/shard_map/nrb,nbc->nrc/dot_general | solution.py:29
  461.5 13.2 %all-gather.11.cloned.1.call-done = f32[128,1,8,256]{3,2,1,0:T(8,128)} async-done(((f32[32,1,8,256]{3,2,1,0:T(8,128)}), f32[128,1,8,256]{3,2,1,0:T(8,128)}) %all-gather.11.cloned.1.call-update) | async-done | bytes 1048592 | tf_op jit(solution)/shard_map/all_gather | solution.py:45
  474.7 3.0 convolution_bitcast_fusion.2
  477.7 8.4 %all-to-all-start.5 = ((f32[32,1,8,256]{3,2,1,0:T(8,128)}), f32[32,1,8,256]{3,2,1,0:T(8,128)S(1)}, u32[]{:S(2)}, u32[]{:S(2)}) async-start(f32[32,1,8,256]{3,2,1,0:T(8,128)} %convolution_bitcast_fusion.2), calls=%async_computation.5 | async-start | bytes 524288 | tf_op jit(solution)/shard_map/all_to_all | solution.py:48
  486.1 6.8 %fusion.47 = f32[32,256,128]{2,1,0:T(8,128)} fusion(f32[32,256,128]{2,1,0:T(8,128)} %fusion.46, f32[32,128,128]{2,1,0:T(8,128)S(1)} %copy-done), kind=kOutput, calls=%fused_computation.95 | convolution fusion | flops 1610612736 | bytes 10485760 | tf_op jit(solution)/shard_map/nrc,nbc->nrb/dot_general | solution.py:30
  493.0 2.1 all-to-all-done.5
  495.8 10.6 %convolution_add_fusion = f32[32,256,128]{2,1,0:T(8,128)} fusion(f32[32,256,128]{2,1,0:T(8,128)} %fusion.47, f32[32,8,128]{2,1,0:T(8,128)S(1)} %copy-done.9, f32[32,8,256]{2,1,0:T(8,128)S(1)} %gather_fusion.9, pred[32]{0:T(512)(128)(4,1)S(1)} %copy-done.15), kind=kOutput, calls=%fused_computation.40 | convolution fusion | flops 101777408 | bytes 8781856 | tf_op jit(solution)/shard_map/ncb,ncr->nrb/dot_general | solution.py:73
  506.4 2.9 gather_fusion.10
  510.1 12.9 %fusion.48 = f32[32,256,128]{2,1,0:T(8,128)} fusion(f32[32,256,128]{2,1,0:T(8,128)} %convolution_add_fusion, f32[32,128,128]{2,1,0:T(8,128)} %param.16), kind=kOutput, calls=%fused_computation.96 | convolution fusion | flops 1610612736 | bytes 10485760 | tf_op jit(solution)/shard_map/nrc,nbc->nrb/dot_general | solution.py:78
  523.0 2.7 pad_maximum_fusion.2
  525.7 12.4 %gather_fusion.11 = f32[128,256,128]{2,1,0:T(8,128)} fusion(f32[40,256,128]{2,1,0:T(8,128)} %pad_maximum_fusion.2, s32[1024]{0:T(1024)S(1)} %pad_clamp_fusion), kind=kCustom, calls=%fused_computation.11.clone | custom fusion | bytes 33554944 | tf_op jit(solution)/shard_map/jit(_take)/gather | solution.py:77
  538.0 23.2 %multiply_reduce_fusion = (f32[]{:T(128)}, f32[]{:T(128)}, f32[32,256,128]{2,1,0:T(8,128)}) fusion(f32[32,256,128]{2,1,0:T(8,128)} %copy-done.1, f32[32,256,128]{2,1,0:T(8,128)} %fusion.48, f32[32,4,128,128]{3,2,1,0:T(8,128)} %param.17, f32[32,4,256,128]{3,2,1,0:T(8,128)} %bitcast.95, pred[32,4]{1,0:T(8,128)(4,1)S(1)} %copy.25), kind=kOutput, calls=%fused_computation.32 | convolution fusion | flops 6451888128 | bytes 37748872 | tf_op jit(solution)/shard_map/nkrc,nkbc->nrb/dot_general | solution.py:79
  561.2 66.1 %all-reduce = (f32[]{:T(128)}, f32[]{:T(128)}) all-reduce(f32[]{:T(128)} %get-tuple-element.8, f32[]{:T(128)} %get-tuple-element.7), channel_id=1, replica_groups=mesh['sub'=32,'grp'=4] {'sub','grp'}, use_global_device_ids=true, to_apply=%region_10.14 | all-reduce | flops 2 | bytes 16 | tf_op jit(solution)/shard_map/psum | solution.py:80
  628.6 8.3 %multiply_add_fusion = f32[32,256,128]{2,1,0:T(8,128)} fusion(f32[32,256,128]{2,1,0:T(8,128)} %convolution_add_fusion, f32[32,256,128]{2,1,0:T(8,128)} %convolution_add_fusion.1, f32[32,256,128]{2,1,0:T(8,128)} %convolution_add_fusion.2, f32[]{:T(128)S(6)} %div.11, f32[]{:T(128)S(6)} %div.10, f32[]{:T(128)S(6)} %div.9), kind=kLoop, calls=%fused_computation.31 | loop fusion | flops 5242880 | bytes 16777228 | tf_op jit(solution)/shard_map/add | solution.py:84
  637.0 2.6 multiply_subtract_fusion
  (79 shorter events, 11.2 us)
Async XLA Ops:
  7.2 28.7 %copy-start = (f32[32,128,128]{2,1,0:T(8,128)S(1)}, f32[32,128,128]{2,1,0:T(8,128)}, u32[]{:S(2)}) copy-start(f32[32,128,128]{2,1,0:T(8,128)} %param.18) | copy-start | bytes 6291460
  7.2 17.3 %copy-start.21 = (s32[32]{0:T(128)S(1)}, s32[32]{0:T(128)}, u32[]{:S(2)}) copy-start(s32[32]{0:T(128)} %param.23) | copy-start | bytes 388
  7.2 26.9 %copy-start.22 = (s32[4]{0:T(128)S(1)}, s32[4]{0:T(128)}, u32[]{:S(2)}) copy-start(s32[4]{0:T(128)} %param.21) | copy-start | bytes 52
  7.2 28.0 %copy-start.13 = (s32[32,4]{0,1:T(4,128)S(1)}, s32[32,4]{0,1:T(4,128)}, u32[]{:S(2)}) copy-start(s32[32,4]{0,1:T(4,128)} %param.22) | copy-start | bytes 1540
  8.7 27.1 %copy-start.16 = (pred[32]{0:T(512)(128)(4,1)}, pred[32]{0:T(512)(128)(4,1)S(1)}, u32[]{:S(2)}) copy-start(pred[32]{0:T(512)(128)(4,1)S(1)} %compare_and_fusion.3) | copy-start | bytes 100
  8.7 27.1 %copy-start.14 = (s32[1024]{0:T(1024)}, s32[1024]{0:T(1024)S(1)}, u32[]{:S(2)}) copy-start(s32[1024]{0:T(1024)S(1)} %pad_clamp_fusion.3) | copy-start | bytes 12292
  15.9 17.5 %all-to-all-start = ((f32[32,1,8,256]{3,2,1,0:T(8,128)}), f32[32,1,8,256]{3,2,1,0:T(8,128)S(1)}, u32[]{:S(2)}, u32[]{:S(2)}) async-start(f32[32,1,8,256]{3,2,1,0:T(8,128)} %select_bitcast_fusion.2), calls=%async_computation | async-start | bytes 524288 | tf_op jit(solution)/shard_map/all_to_all | solution.py:43
  24.4 31.4 %all-gather.7.cloned.1.call-start = ((), (), s32[]{:S(2)}) async-start(), calls=%async_computation.6 | async-start | bytes 1310720 | tf_op jit(solution)/shard_map/all_gather | solution.py:45
  33.3 0.7 copy-start.12
  41.5 14.4 %copy-start.8 = (f32[1,256,1024]{2,1,0:T(8,128)S(1)}, f32[1,256,1024]{2,1,0:T(8,128)}, u32[]{:S(2)}) copy-start(f32[1,256,1024]{2,1,0:T(8,128)} %param.20) | copy-start | bytes 3145732
  41.5 37.1 %copy-start.9 = (f32[32,8,128]{2,1,0:T(8,128)S(1)}, f32[32,8,128]{2,1,0:T(8,128)}, u32[]{:S(2)}) copy-start(f32[32,8,128]{2,1,0:T(8,128)} %param.19) | copy-start | bytes 393220
  58.9 17.3 %all-to-all-start.1 = ((f32[32,1,8,256]{3,2,1,0:T(8,128)}), f32[32,1,8,256]{3,2,1,0:T(8,128)S(1)}, u32[]{:S(2)}, u32[]{:S(2)}) async-start(f32[32,1,8,256]{3,2,1,0:T(8,128)} %convolution_bitcast_fusion.4), calls=%async_computation.1 | async-start | bytes 524288 | tf_op jit(solution)/shard_map/all_to_all | solution.py:48
  67.3 204.0 %all-gather.9.cloned.1.call-start = ((), (), s32[]{:S(2)}) async-start(), calls=%async_computation.7 | async-start | bytes 1310720 | tf_op jit(solution)/shard_map/all_gather | solution.py:45
  76.2 0.7 copy-start.10
  78.6 14.3 %copy-start.18 = (pred[4]{0:T(512)(128)(4,1)S(1)}, pred[4]{0:T(512)(128)(4,1)}, u32[]{:S(2)}) copy-start(pred[4]{0:T(512)(128)(4,1)} %compare_and_fusion.1) | copy-start | bytes 16
  78.6 16.8 %copy-start.20 = (s32[128]{0:T(128)S(1)}, s32[128]{0:T(128)}, u32[]{:S(2)}) copy-start(s32[128]{0:T(128)} %reshape.190) | copy-start | bytes 1540
  94.9 13.3 %collective-permute-start = (f32[4,256,128]{2,1,0:T(8,128)}, f32[4,256,128]{2,1,0:T(8,128)}, u32[]{:S(2)}, u32[]{:S(2)}) collective-permute-start(f32[4,256,128]{2,1,0:T(8,128)} %broadcast_select_fusion.2), channel_id=1, source_target_pairs={{0,4},{4,8},{8,12},{12,16},{16,20},{20,24},{24,28},{28,32},{32,36}... | collective-permute-start | bytes 1572872 | tf_op jit(solution)/shard_map/ppermute | solution.py:19
  95.3 12.8 %collective-permute-start.1 = (f32[4,256,128]{2,1,0:T(8,128)}, f32[4,256,128]{2,1,0:T(8,128)}, u32[]{:S(2)}, u32[]{:S(2)}) collective-permute-start(f32[4,256,128]{2,1,0:T(8,128)} %broadcast_select_fusion.2), channel_id=1, source_target_pairs={{4,0},{8,4},{12,8},{16,12},{20,16},{24,20},{28,24},{32,28},{36,32}... | collective-permute-start | bytes 1572872 | tf_op jit(solution)/shard_map/ppermute | solution.py:21
  95.5 12.6 %copy-start.4 = (f32[32,256,128]{2,1,0:T(8,128)S(1)}, f32[32,256,128]{2,1,0:T(8,128)}, u32[]{:S(2)}) copy-start(f32[32,256,128]{2,1,0:T(8,128)} %convolution_add_fusion.2) | copy-start | bytes 12582916
  229.6 2.0 copy-start.3
  231.6 5.0 copy-start.17
  274.3 17.3 %all-to-all-start.3 = ((f32[32,1,8,256]{3,2,1,0:T(8,128)}), f32[32,1,8,256]{3,2,1,0:T(8,128)S(1)}, u32[]{:S(2)}, u32[]{:S(2)}) async-start(f32[32,1,8,256]{3,2,1,0:T(8,128)} %convolution_bitcast_fusion.3), calls=%async_computation.3 | async-start | bytes 524288 | tf_op jit(solution)/shard_map/all_to_all | solution.py:48
  282.8 11.2 %copy-start.15 = (pred[32]{0:T(512)(128)(4,1)S(1)}, pred[32]{0:T(512)(128)(4,1)}, u32[]{:S(2)}) copy-start(pred[32]{0:T(512)(128)(4,1)} %compare_and_fusion.2) | copy-start | bytes 100
  282.8 191.9 %all-gather.11.cloned.1.call-start = ((), (), s32[]{:S(2)}) async-start(), calls=%async_computation.8 | async-start | bytes 1310720 | tf_op jit(solution)/shard_map/all_gather | solution.py:45
  291.7 0.7 copy-start.11
  309.6 13.8 %copy-start.5 = (f32[32,256,128]{2,1,0:T(8,128)S(1)}, f32[32,256,128]{2,1,0:T(8,128)}, u32[]{:S(2)}) copy-start(f32[32,256,128]{2,1,0:T(8,128)} %convolution_add_fusion.1) | copy-start | bytes 12582916
  309.6 13.7 %collective-permute-start.2 = (f32[4,256,128]{2,1,0:T(8,128)S(1)}, f32[4,256,128]{2,1,0:T(8,128)S(1)}, u32[]{:S(2)}, u32[]{:S(2)}) collective-permute-start(f32[4,256,128]{2,1,0:T(8,128)S(1)} %broadcast_select_fusion.1), channel_id=1, source_target_pairs={{0,4},{4,8},{8,12},{12,16},{16,20},{20,24},{24,28},{28,32},{32,36}... | collective-permute-start | bytes 1572872 | tf_op jit(solution)/shard_map/ppermute | solution.py:19
  310.1 13.3 %collective-permute-start.3 = (f32[4,256,128]{2,1,0:T(8,128)S(1)}, f32[4,256,128]{2,1,0:T(8,128)S(1)}, u32[]{:S(2)}, u32[]{:S(2)}) collective-permute-start(f32[4,256,128]{2,1,0:T(8,128)S(1)} %broadcast_select_fusion.1), channel_id=1, source_target_pairs={{4,0},{8,4},{12,8},{16,12},{20,16},{24,20},{28,24},{32,28},{36,32}... | collective-permute-start | bytes 1572872 | tf_op jit(solution)/shard_map/ppermute | solution.py:21
  433.0 2.0 copy-start.1
  477.7 17.3 %all-to-all-start.5 = ((f32[32,1,8,256]{3,2,1,0:T(8,128)}), f32[32,1,8,256]{3,2,1,0:T(8,128)S(1)}, u32[]{:S(2)}, u32[]{:S(2)}) async-start(f32[32,1,8,256]{3,2,1,0:T(8,128)} %convolution_bitcast_fusion.2), calls=%async_computation.5 | async-start | bytes 524288 | tf_op jit(solution)/shard_map/all_to_all | solution.py:48
  495.8 13.5 %copy-start.19 = (pred[4]{0:T(512)(128)(4,1)S(1)}, pred[4]{0:T(512)(128)(4,1)}, u32[]{:S(2)}) copy-start(pred[4]{0:T(512)(128)(4,1)} %compare_and_fusion.1) | copy-start | bytes 16
  509.4 13.7 %copy-start.6 = (f32[32,256,128]{2,1,0:T(8,128)S(1)}, f32[32,256,128]{2,1,0:T(8,128)}, u32[]{:S(2)}) copy-start(f32[32,256,128]{2,1,0:T(8,128)} %convolution_add_fusion) | copy-start | bytes 12582916
  509.4 13.6 %collective-permute-start.4 = (f32[4,256,128]{2,1,0:T(8,128)S(1)}, f32[4,256,128]{2,1,0:T(8,128)S(1)}, u32[]{:S(2)}, u32[]{:S(2)}) collective-permute-start(f32[4,256,128]{2,1,0:T(8,128)S(1)} %broadcast_select_fusion), channel_id=1, source_target_pairs={{0,4},{4,8},{8,12},{12,16},{16,20},{20,24},{24,28},{28,32},{32,36}... | collective-permute-start | bytes 1572872 | tf_op jit(solution)/shard_map/ppermute | solution.py:19
  509.9 13.2 %collective-permute-start.5 = (f32[4,256,128]{2,1,0:T(8,128)S(1)}, f32[4,256,128]{2,1,0:T(8,128)S(1)}, u32[]{:S(2)}, u32[]{:S(2)}) collective-permute-start(f32[4,256,128]{2,1,0:T(8,128)S(1)} %broadcast_select_fusion), channel_id=1, source_target_pairs={{4,0},{8,4},{12,8},{16,12},{20,16},{24,20},{28,24},{32,28},{36,32}... | collective-permute-start | bytes 1572872 | tf_op jit(solution)/shard_map/ppermute | solution.py:21
  628.6 8.4 %copy-start.2 = (f32[32,256,128]{2,1,0:T(8,128)S(1)}, f32[32,256,128]{2,1,0:T(8,128)}, u32[]{:S(2)}) copy-start(f32[32,256,128]{2,1,0:T(8,128)} %copy-done.1) | copy-start | bytes 12582916
  628.6 8.4 %copy-start.7 = (f32[32,256,128]{2,1,0:T(8,128)S(1)}, f32[32,256,128]{2,1,0:T(8,128)}, u32[]{:S(2)}) copy-start(f32[32,256,128]{2,1,0:T(8,128)} %get-tuple-element.21) | copy-start | bytes 12582916
Sparse Core Ops, SparseCore 0:
  34.2 21.6 all-gather.6
  251.5 19.8 all-gather.8
  454.8 19.8 all-gather.10
where the time goes:
time: 655 us; the launch traced here: 647 us
  blocking collectives  236 us (36%)
  matrix products  200 us (31%)
  local copies, waits for them, and re-layouts  62.4 us (10%)
  waiting for transfers between devices  52.1 us (8%)
  other arithmetic  41 us (6%)
  starting transfers between devices  36.5 us (6%)
  between operations  18.4 us (3%)
    psum x3, blocking collectives, local(): lax.psum((jnp.sum(image * residual), jnp.sum(image * image)), ('sub', 'gr...  209 us
    dot_general x3, matrix products, local(): jnp.einsum('nkrc,nkbc->nrb', picked, couplings, precision=HI)  69.5 us
    dot_general x3, matrix products, local(): image = jnp.einsum('nrc,nbc->nrb', direction, diag_blocks, precision=HI)  38.3 us
    gather x3, local copies, waits for them, and re-layouts, local(): picked = jnp.take(extended, neighbours, axis=0)  37.1 us
    all_gather x3, waiting for transfers between devices, coarse_solve(): piece = lax.all_gather(arrived[None], 'grp', axis=0, tiled=True)  35.5 us
    dot_general x3, matrix products, local(): coarse = jnp.einsum('ncb,ncr->nrb', prolong, coarse_sol, precision=HI)  31.9 us
    all_to_all x2, blocking collectives, coarse_solve(): lax.all_to_all(parcel, 'sub', split_axis=0, concat_axis=0, tiled=True)  27.2 us
    all_to_all x3, starting transfers between devices, coarse_solve(): lax.all_to_all(solved.reshape(groups, per, ncoarse, nrhs), 'sub', split_a...  25.3 us
  transfers between devices with their start and end apart: 13, of which 7 were waited for; matrix products, arithmetic and copies ran while one was open for 13% of the time, Pallas kernels for 0%

commit v1 on v0

v1 whole, which is shorter than its diff:
```python
import functools

import jax
import jax.numpy as jnp
from jax import lax
from jax.experimental import pallas as pl
from jax.experimental.pallas import tpu as pltpu
from jax.sharding import PartitionSpec as P

F32 = jnp.float32
BF16 = jnp.bfloat16
TILES = 7
VMEM = 60 * 1024 * 1024
SMALL = 16 * 1024 * 1024


def nn(a, b):
    return lax.dot_general(a, b, (((1,), (0,)), ((), ())), preferred_element_type=F32)


def nt(a, b):
    return lax.dot_general(a, b, (((1,), (1,)), ((), ())), preferred_element_type=F32)


def tn(a, b):
    return lax.dot_general(a, b, (((0,), (0,)), ((), ())), preferred_element_type=F32)


def parts(x):
    head = x.astype(BF16)
    return head, (x - head.astype(F32)).astype(BF16)


def wide(x):
    return jnp.concatenate(parts(x), axis=1)


def fold(x):
    half = x.shape[1] // 2
    return x[:, :half] + x[:, half:]


def weights_nt(w):
    h, l = parts(w)
    return jnp.concatenate([jnp.concatenate([h, h], 1), jnp.concatenate([l, l], 1)], 0)


def weights_nn(w):
    h, l = parts(w)
    row = jnp.concatenate([h, l], 1)
    return jnp.concatenate([row, row], 0)


def rows_by(p):
    return weights_nt(p)


def fold_rows(x):
    half = x.shape[0] // 2
    return x[:half] + x[half:]


def cost(flops, nbytes):
    return pl.CostEstimate(flops=int(flops), bytes_accessed=int(nbytes), transcendentals=0)


SMEM = pl.BlockSpec(memory_space=pltpu.SMEM)
ANY = pl.BlockSpec(memory_space=pl.ANY)
INVMEM = pl.BlockSpec(memory_space=pltpu.VMEM)


def whole(x):
    zeros = (0,) * len(x.shape)
    return pl.BlockSpec(x.shape, lambda *_: zeros)


def lead(x, block, at=lambda i: i):
    tail = (0,) * (len(x.shape) - 1)
    return pl.BlockSpec((block,) + tuple(x.shape[1:]), lambda i, *_: (at(i),) + tail)


def shape_of(shape, kind=F32):
    return jax.ShapeDtypeStruct(shape, kind)


def call(kernel, name, grid, arrays, in_specs, outs, out_specs, flops, scratch=(), limit=VMEM):
    moved = sum(x.nbytes for x in arrays) + sum(x.size * x.dtype.itemsize for x in outs)
    return pl.pallas_call(
        kernel,
        grid=grid,
        in_specs=in_specs,
        out_specs=out_specs,
        out_shape=outs,
        scratch_shapes=list(scratch),
        compiler_params=pltpu.CompilerParams(vmem_limit_bytes=limit),
        cost_estimate=cost(flops, moved),
        name=name,
    )(*arrays)


def each(count, step, body):
    def some(i, _):
        for j in range(step):
            body(i * step + j)
        return 0

    lax.fori_loop(0, count // step, some, 0)


def gathered(ret, cpos, nbr, n):
    tiles = []
    for k in range(5):
        t = cpos[n] if k == 0 else cpos[nbr[n * 4 + k - 1]]
        tiles.append(jnp.concatenate([ret[t], ret[t + 1]], axis=1))
    c = jnp.concatenate(tiles, axis=0)
    h = c.astype(BF16).astype(F32)
    pad = jnp.zeros((8, c.shape[1]), F32)
    return jnp.concatenate([h, c - h, h, pad], axis=0).astype(BF16)


def alpha_of(ret, blocks):
    total = ret[TILES - 1]
    for q in range(1, blocks):
        total = total + ret[q * TILES + TILES - 1]
    return total[0:1, 0:1] / total[1:2, 0:1]


def invert(pick, inv):
    def put(q, _):
        inv[pick[q]] = q
        return 0

    lax.fori_loop(0, pick.shape[0], put, 0)


def first_kernel(pick, r_ref, p_ref, send_ref, inv_ref, *, step):
    i = pl.program_id(0)

    @pl.when(i == 0)
    def _():
        invert(pick, inv_ref)

    for j in range(step):
        rhs = fold_rows(nt(rows_by(p_ref[j]), wide(r_ref[j])))
        slot = inv_ref[i * step + j]
        for g in range(send_ref.shape[0]):
            send_ref[g, slot] = rhs


def first_rhs(pick, r, p, groups):
    nb, nr, b = r.shape
    nc = p.shape[1]
    step = 8
    send = shape_of((groups, nb, nc, nr))
    return call(
        functools.partial(first_kernel, step=step),
        "first_rhs",
        (nb // step,),
        [pick, r, p],
        [SMEM, lead(r, step), lead(p, step)],
        [send, shape_of((nb,), jnp.int32)],
        [whole(send), SMEM],
        2 * 16 * 256 * 256 * nb,
    )


def fine_block(v, f):
    inner = fold(nn(wide(v), weights_nn(f)))
    return fold(nt(wide(inner), weights_nt(f)))


def sent_first_kernel(send, inv, v_ref, f_ref, p_ref, out_ref, v, f, p, sems):
    count = send.shape[0]
    nr = v.shape[1]
    nc = p.shape[1]
    copies = []
    for j in range(count):
        for k, (src, dst) in enumerate(((v_ref, v), (f_ref, f), (p_ref, p))):
            copies.append(pltpu.make_async_copy(src.at[send[j]], dst.at[j], sems.at[k, j]))
    for c in copies:
        c.start()
    for c in copies:
        c.wait()
    for j in range(count):
        out_ref[j, :nr] = fine_block(v[j], f[j])
        out_ref[j, nr : nr + nc] = p[j]
        out_ref[j, nr + nc :] = jnp.full((8, p.shape[2]), inv[send[j]].astype(F32))


def fine_sent(send, inv, v, f, p):
    _, nr, b = v.shape
    nc = p.shape[1]
    count = send.shape[0]
    return call(
        sent_first_kernel,
        "fine_sent",
        (),
        [send, inv, v, f, p],
        [SMEM, SMEM, ANY, ANY, ANY],
        [shape_of((count, nr + nc + 8, b))],
        [INVMEM],
        4 * 256**3 * count,
        [
            pltpu.VMEM((count, nr, b), F32),
            pltpu.VMEM((count, b, b), F32),
            pltpu.VMEM((count, nc, b), F32),
            pltpu.SemaphoreType.DMA((3, count)),
        ],
    )[0]


FINE_STEP = 8
OP_STEP = 4


def fine_operator_kernel(nbr, v_ref, fac_ref, lo_ref, up_ref, d_ref, w_ref, p_ref, *refs, setup, paf):
    refs = list(refs)
    f_ref, af_ref = refs[:2]
    refs = refs[2:]
    paf_ref = refs.pop(0) if paf else None
    if setup:
        g_ref, h_ref = refs[:2]
        refs = refs[2:]
    ext = refs.pop(0)
    kept = refs.pop(0) if paf else None
    if setup:
        pext, grows = refs
    i = pl.program_id(0)
    nb = p_ref.shape[0]
    nr, nc = v_ref.shape[1], p_ref.shape[1]
    halo = lo_ref.shape[0]
    fine_steps = nb // FINE_STEP

    @pl.when(i < fine_steps)
    def _():
        for j in range(FINE_STEP):
            f2 = wide(fine_block(v_ref[j], fac_ref[j]))
            f_ref[j] = f2
            ext[i * FINE_STEP + j] = f2

    @pl.when(i == fine_steps - 1)
    def _():
        for j in range(halo):
            ext[nb + j] = wide(lo_ref[j, :nr])
            ext[nb + halo + j] = wide(up_ref[j, :nr])
        if setup:
            pext[pl.ds(0, nb)] = p_ref[...]
            pext[pl.ds(nb, halo)] = lo_ref[:, nr : nr + nc]
            pext[pl.ds(nb + halo, halo)] = up_ref[:, nr : nr + nc]

    def products(at):
        for j in range(OP_STEP):
            n = at * OP_STEP + j
            p = p_ref[n]
            paf_ref[n] = fold_rows(nt(wide(kept[n]), rows_by(p)).T)
            if setup:
                g = grows[n]
                gh = g.astype(BF16).astype(F32)
                pad = jnp.zeros((8, g.shape[1]), F32)
                g_ref[n] = jnp.concatenate([gh, gh, g - gh, pad], axis=0).astype(BF16)
                thrice = jnp.concatenate([g, g, g, pad], axis=0)
                h = fold_rows(nt(rows_by(p), wide(thrice)))
                hh = h.astype(BF16).astype(F32)
                lane = lax.broadcasted_iota(jnp.int32, h.shape, 1)
                h_ref[n] = jnp.where(lane < 80, hh, h - hh)

    @pl.when(i >= fine_steps)
    def _():
        at = i - fine_steps
        if paf:
            products(jnp.maximum(at - 1, 0))
        for j in range(OP_STEP):
            n = at * OP_STEP + j
            fields = []
            weights = []
            rows = []
            for k in range(5):
                e = n if k == 0 else nbr[n * 4 + k - 1]
                weights.append(weights_nt(d_ref[j] if k == 0 else w_ref[j, k - 1]))
                fields.append(ext[e])
                if setup:
                    p = pext[e]
                    ph = p.astype(BF16).astype(F32)
                    row = [jnp.zeros((nc, 2 * p.shape[1]), F32)] * 5
                    row[k] = jnp.concatenate([ph, p - ph], axis=1)
                    rows.append(jnp.concatenate(row, axis=1))
            lhs = jnp.concatenate(fields, axis=1)
            if setup:
                rows = jnp.concatenate(rows + [jnp.zeros_like(rows[0])], axis=0).astype(BF16)
                lhs = jnp.concatenate([lhs, rows], axis=0)
            got = fold(nt(lhs, jnp.concatenate(weights, axis=1)))
            if setup:
                grows[n] = got[nr : nr + 5 * nc]
                got = got[:nr]
            af_ref[j] = got
            if paf:
                kept[n] = got

    if paf:

        @pl.when(i == pl.num_programs(0) - 1)
        def _():
            products(nb // OP_STEP - 1)


def fine_operator(nbr, v, fac, lo, up, d, w, p, setup=False, paf=True):
    nb, nr, b = v.shape
    nc = p.shape[1]
    fine_steps = nb // FINE_STEP

    def early(i):
        return jnp.minimum(i, fine_steps - 1)

    def late(i):
        return jnp.maximum(i - fine_steps, 0)

    places = nb + 2 * lo.shape[0]
    f2 = shape_of((nb, nr, 2 * b), BF16)
    af = shape_of((nb, nr, b))
    outs = [f2, af]
    out_specs = [lead(f2, FINE_STEP, early), lead(af, OP_STEP, late)]
    scratch = [pltpu.VMEM((places, nr, 2 * b), BF16)]
    if paf:
        more = [shape_of((nb, nc, nr))]
        scratch.append(pltpu.VMEM((nb, nr, b), F32))
        if setup:
            more += [shape_of((nb, b, b), BF16), shape_of((nb, nc, b))]
            scratch += [pltpu.VMEM((places, nc, b), F32), pltpu.VMEM((nb, 5 * nc, b), F32)]
        outs += more
        out_specs += [whole(x) for x in more]
    return call(
        functools.partial(fine_operator_kernel, setup=setup, paf=paf),
        "fine_operator",
        (fine_steps + nb // OP_STEP,),
        [nbr, v, fac, lo, up, d, w, p],
        [
            SMEM,
            lead(v, FINE_STEP, early),
            lead(fac, FINE_STEP, early),
            whole(lo),
            whole(up),
            lead(d, OP_STEP, late),
            lead(w, OP_STEP, late),
            whole(p),
        ],
        outs,
        out_specs,
        14 * 256**3 * nb,
        scratch,
    )


def solve_kernel(v_ref, c_ref, *refs):
    *sums, out_ref, v, res, sems, sem = refs
    steps = v.shape[0]
    copies = [pltpu.make_async_copy(v_ref.at[k], v.at[k], sems.at[k]) for k in range(steps)]
    for c in copies:
        c.start()
    size = v.shape[1]
    sol = None
    for k in range(steps):
        ch, cl = parts(c_ref[0, :, k * size : (k + 1) * size])
        copies[k].wait()
        vh, vl = parts(v[k])
        term = nn(ch, vh) + nn(ch, vl) + nn(cl, vh)
        sol = term if sol is None else sol + term
    ns = res.shape[0]
    half = sol.shape[1] // 2
    total = sums[0][...] + sums[1][...] if sums else jnp.zeros((8, half), F32)
    for s in range(ns):
        rows = sol[8 * s : 8 * s + 8]
        for place, to in ((0, s), (1, (s + 1) % ns), (2, (s - 1) % ns)):
            res[to, 2 * place] = rows[:, :half]
            res[to, 2 * place + 1] = rows[:, half:]
        res[s, TILES - 1] = total
    out = pltpu.make_async_copy(res, out_ref, sem)
    out.start()
    out.wait()


def solve(vec, inverse, ns, sums):
    steps, k, nr = vec.shape
    shape = (ns, TILES, 8, nr // 2)
    return call(
        solve_kernel,
        "coarse_solve",
        (),
        [vec, inverse, *sums],
        [ANY, INVMEM] + [INVMEM] * len(sums),
        [shape_of(shape)],
        [ANY],
        2 * 3 * 256 * k * steps * nr,
        [
            pltpu.VMEM(vec.shape, F32),
            pltpu.VMEM(shape, F32),
            pltpu.SemaphoreType.DMA((steps,)),
            pltpu.SemaphoreType.DMA,
        ],
    )[0]


def next_kernel(cpos, nbr, ret_ref, paf_ref, h_ref, *refs):
    nb = paf_ref.shape[0]
    *old, new_ref, send_ref, slots, sems = refs
    alpha = alpha_of(ret_ref, nb) if old else None

    def one(n):
        c = gathered(ret_ref, cpos, nbr, n)
        rhs = paf_ref[n] + nn(h_ref[n].astype(BF16), c)
        if old:
            rhs = old[0][n] - alpha * rhs
        new_ref[n] = rhs
        slots[lax.div(cpos[n], TILES)] = rhs

    each(nb, 8, one)
    copies = [
        pltpu.make_async_copy(slots, send_ref.at[g], sems.at[g]) for g in range(send_ref.shape[0])
    ]
    for c in copies:
        c.start()
    for c in copies:
        c.wait()


def next_rhs(cpos, nbr, ret, paf, h, groups, old=None):
    nb, nc, nr = paf.shape
    ins = [ret, paf, h] + ([] if old is None else [old])
    return call(
        next_kernel,
        "next_rhs",
        (),
        [cpos, nbr] + ins,
        [SMEM, SMEM] + [INVMEM] * len(ins),
        [shape_of((nb, nc, nr)), shape_of((groups, nb, nc, nr))],
        [INVMEM, ANY],
        2 * 16 * 256 * 128 * nb,
        [pltpu.VMEM((nb, nc, nr), F32), pltpu.SemaphoreType.DMA((groups,))],
    )


def image_kernel(cpos, nbr, *refs, step, later, sent):
    refs = list(refs)
    if sent:
        send = refs.pop(0)
    ret_ref, g_ref, af_ref, r_ref = refs[:4]
    refs = refs[4:]
    old_ref = refs.pop(0) if later else None
    fac_ref = refs.pop(0) if sent else None
    w_ref = refs.pop(0)
    new_r_ref = refs.pop(0) if later else None
    sum_ref = refs.pop(0)
    sent_ref = refs.pop(0) if sent else None
    acc = refs.pop(0)
    if sent:
        kept, fac, sems = refs
    i = pl.program_id(0)
    last = pl.num_programs(0) - 1

    def fetch(j):
        return pltpu.make_async_copy(fac_ref.at[send[j]], fac.at[j], sems.at[j])

    @pl.when(i == 0)
    def _():
        acc[...] = jnp.zeros_like(acc)
        if sent:
            for j in range(fac.shape[0]):
                fetch(j).start()

    if later:
        alpha = alpha_of(ret_ref, cpos.shape[0] - 8)
    upper = acc[0]
    lower = acc[1]
    for j in range(step):
        n = i * step + j
        c = gathered(ret_ref, cpos, nbr, n)
        w = af_ref[j] + tn(c, g_ref[j])
        r = r_ref[j]
        if later:
            old = old_ref[j]
            w = old - alpha * w
            r = r - alpha * old
            new_r_ref[j] = r
        w_ref[j] = w
        if sent:
            kept[n] = w
        upper += jnp.sum((w * r).reshape(-1, 8, w.shape[1]), axis=0)
        lower += jnp.sum((w * w).reshape(-1, 8, w.shape[1]), axis=0)
    acc[0] = upper
    acc[1] = lower

    @pl.when(i == last)
    def _():
        up = jnp.sum(acc[0], keepdims=True)
        low = jnp.sum(acc[1], keepdims=True)
        row = lax.broadcasted_iota(jnp.int32, sum_ref.shape, 0)
        sum_ref[...] = jnp.where(row == 0, up, low)
        if sent:
            for j in range(fac.shape[0]):
                fetch(j).wait()
            for j in range(fac.shape[0]):
                sent_ref[j] = fine_block(kept[send[j]], fac[j])


def image_of(cpos, nbr, ret, g, af, r, old=None, send=None, fac=None):
    nb, nr, b = af.shape
    step = 4
    later = old is not None
    sent = send is not None
    big = lead(af, step)
    ins = [cpos, nbr]
    specs = [SMEM, SMEM]
    if sent:
        ins.append(send)
        specs.append(SMEM)
    ins += [ret, g, af, r]
    specs += [whole(ret), lead(g, step), big, big]
    if later:
        ins.append(old)
        specs.append(big)
    outs = [af] * (2 if later else 1)
    out_specs = [big] * len(outs)
    sums = shape_of((8, b))
    outs.append(sums)
    out_specs.append(whole(sums))
    scratch = [pltpu.VMEM((2, 8, b), F32)]
    if sent:
        ins.append(fac)
        specs.append(ANY)
        count = send.shape[0]
        sent_blocks = shape_of((count, nr, b))
        outs.append(sent_blocks)
        out_specs.append(whole(sent_blocks))
        scratch += [
            pltpu.VMEM((nb, nr, b), F32),
            pltpu.VMEM((count, b, b), F32),
            pltpu.SemaphoreType.DMA((count,)),
        ]
    return call(
        functools.partial(image_kernel, step=step, later=later, sent=sent),
        "image",
        (nb // step,),
        ins,
        specs,
        [shape_of(x.shape) for x in outs],
        out_specs,
        2 * 256 * 128 * 128 * nb,
        scratch,
    )


def combine_kernel(cpos, r0_ref, r1_ref, r2_ref, p_ref, f0_ref, f1_ref, f2_ref, s_ref, d_ref, *, step):
    i = pl.program_id(0)
    nb = cpos.shape[0] - 8
    a0 = alpha_of(r1_ref, nb)
    a1 = alpha_of(r2_ref, nb)
    for j in range(step):
        p = p_ref[j]
        ph = p.astype(BF16).astype(F32)
        p3 = jnp.concatenate([ph, ph, p - ph, jnp.zeros_like(p)], axis=0).astype(BF16)
        t = cpos[i * step + j]
        found = []
        for ret, f_ref in ((r0_ref, f0_ref), (r1_ref, f1_ref), (r2_ref, f2_ref)):
            c = jnp.concatenate([ret[t], ret[t + 1]], axis=1)
            h = c.astype(BF16).astype(F32)
            c3 = jnp.concatenate([h, c - h, h, jnp.zeros_like(h)], axis=0).astype(BF16)
            fine = f_ref[j].astype(F32)
            found.append(fold(fine) + tn(c3, p3))
        d0 = found[0]
        d1 = d0 - a0 * found[1]
        s_ref[j] = a0 * d0 + a1 * d1
        d_ref[j] = d1 - a1 * found[2]


def combine(cpos, rets, p, fs):
    nb, _, b = p.shape
    nr = fs[0].shape[1]
    step = 4
    out = shape_of((nb, nr, b))
    return call(
        functools.partial(combine_kernel, step=step),
        "combine",
        (nb // step,),
        [cpos, *rets, p, *fs],
        [SMEM] + [whole(x) for x in rets] + [lead(p, step)] + [lead(f, step) for f in fs],
        [out, out],
        [lead(out, step)] * 2,
        2 * 3 * 256 * 128 * 128 * nb,
    )


def shifted(x, axis, by):
    count = lax.axis_size(axis)
    return lax.ppermute(x, axis, [(i, (i + by) % count) for i in range(count)])


def both_ways(x):
    return shifted(x, "sub", 1), shifted(x, "sub", -1)


def local(
    right_side,
    diag_blocks,
    couplings,
    factors,
    prolong,
    coarse_inverse,
    intersection_send,
    neighbours,
    coarse_pick,
):
    nb, nr, b = right_side.shape
    nc = prolong.shape[1]
    ns = lax.axis_size("sub")
    ng = lax.axis_size("grp")
    nbr = neighbours.reshape(-1)

    def exchange(send):
        flat = send.reshape(ng * nb, nc, nr)
        got = lax.all_to_all(flat, ("grp", "sub"), split_axis=0, concat_axis=0, tiled=True)
        return got.reshape(ng, nb * nc, nr)

    def coarse(vec, sums):
        out = solve(vec, coarse_inverse, ns, sums)
        back = lax.all_to_all(out, "sub", split_axis=0, concat_axis=0, tiled=True)
        return back.reshape(ns * TILES, 8, nr // 2)

    def over_grp(sums):
        sums = sums + lax.ppermute(sums, "grp", [(i, i ^ 1) for i in range(ng)])
        return sums, lax.ppermute(sums, "grp", [(i, ng - 1 - i) for i in range(ng)])

    def places(x):
        return x[:, nr + nc, 0].astype(jnp.int32) * TILES

    weights = (diag_blocks, couplings, prolong)
    send, inv = first_rhs(coarse_pick, right_side, prolong, ng)
    vec0 = exchange(send)
    lo, up = both_ways(fine_sent(intersection_send, inv, right_side, factors, prolong))
    cpos = jnp.concatenate([inv * TILES, places(lo) + 2, places(up) + 4])
    f0, af0, paf0, g, h = fine_operator(nbr, right_side, factors, lo, up, *weights, setup=True)
    ret0 = coarse(vec0, ())

    pw0, send = next_rhs(cpos, nbr, ret0, paf0, h, ng)
    vec1 = exchange(send)
    w0, sums, sent = image_of(
        cpos, nbr, ret0, g, af0, right_side, None, intersection_send, factors
    )
    lo, up = both_ways(sent)
    sums = over_grp(sums)
    f1, af1, paf1 = fine_operator(nbr, w0, factors, lo, up, *weights)
    ret1 = coarse(vec1, sums)

    _, send = next_rhs(cpos, nbr, ret1, paf1, h, ng, pw0)
    vec2 = exchange(send)
    w1, r1, sums, sent = image_of(
        cpos, nbr, ret1, g, af1, right_side, w0, intersection_send, factors
    )
    lo, up = both_ways(sent)
    sums = over_grp(sums)
    f2, af2 = fine_operator(nbr, w1, factors, lo, up, *weights, paf=False)
    ret2 = coarse(vec2, sums)

    w2, r2, sums = image_of(cpos, nbr, ret2, g, af2, r1, w1)
    every = jnp.broadcast_to(sums[None, :1], (ns * ng, 1, b))
    every = jnp.concatenate([every, jnp.broadcast_to(sums[None, 1:2], (ns * ng, 1, b))], axis=1)
    every = lax.all_to_all(every, ("grp", "sub"), split_axis=0, concat_axis=0, tiled=True)
    s2, d2 = combine(cpos, (ret0, ret1, ret2), prolong, (f0, f1, f2))
    total = jnp.sum(every[:, :, 0], axis=0)
    alpha = total[0] / total[1]
    return s2 + alpha * d2, r2 - alpha * w2


def solution(mesh):
    return jax.shard_map(
        local,
        mesh=mesh,
        in_specs=(
            P(("sub", "grp"), None, None),
            P(("sub", "grp"), None, None),
            P(("sub", "grp"), None, None, None),
            P(("sub", "grp"), None, None),
            P(("sub", "grp"), None, None),
            P("sub", "grp", None),
            P(("sub", "grp")),
            P(("sub", "grp"), None),
            P(("sub", "grp")),
        ),
        out_specs=(P(("sub", "grp"), None, None), P(("sub", "grp"), None, None)),
        check_vma=False,
    )
```

time: 655 us -> 261 us (0.40)
  blocking collectives: 236 us -> 0 us
  matrix products: 200 us -> 0 us
  Pallas kernels: 0 us -> 132 us
  local copies, waits for them, and re-layouts: 62.4 us -> 10.6 us
  starting transfers between devices: 36.5 us -> 79.7 us
  waiting for transfers between devices: 52.1 us -> 19.4 us
  other arithmetic: 41 us -> 14.3 us
  between operations: 18.4 us -> 2.29 us
    psum x3 -> x0, blocking collectives: 209 us -> none  [local(): lax.psum((jnp.sum(image * residual), jnp.sum(image * image)), ('sub', 'gr...]
    dot_general x21 -> x0, matrix products: 200 us -> none  [the longest x3 69.5 us: local(): jnp.einsum('nkrc,nkbc->nrb', picked, couplings, precision=HI)]
    pallas_call x0 -> x14, Pallas kernels: none -> 132 us  [call(): pl.pallas_call(kernel, grid=grid, in_specs=in_specs, out_specs=out_specs,...]
    gather x12 -> x0, local copies, waits for them, and re-layouts: 54.7 us -> none  [the longest x3 37.1 us: local(): picked = jnp.take(extended, neighbours, axis=0)]
    all_gather x3 -> x0, waiting for transfers between devices: 35.5 us -> none  [coarse_solve(): piece = lax.all_gather(arrived[None], 'grp', axis=0, tiled=True)]
    all_to_all x4 -> x7, starting transfers between devices: 33.9 us -> 66 us  [the longest x3 30.5 us: exchange(): lax.all_to_all(flat, ('grp', 'sub'), split_axis=0, concat_axis=0, tiled=T...]
    all_to_all x2 -> x0, blocking collectives: 27.2 us -> none  [coarse_solve(): lax.all_to_all(parcel, 'sub', split_axis=0, concat_axis=0, tiled=True)]
    ppermute x6 -> x10, waiting for transfers between devices: 0.02 us -> 17.3 us  [the longest x6 11.3 us: shifted(): return lax.ppermute(x, axis, [(i, (i + by) % count) for i in range(count)])]
  transfers between devices with their start and end apart: 13 -> 17, of which waited for: 7 -> 6; matrix products, arithmetic and copies ran while one was open for 13% -> 1% of each run, Pallas kernels for 0% -> 42%
where the time goes in v1:
time: 261 us; the launch traced here: 259 us
  Pallas kernels  132 us (51%)
  starting transfers between devices  79.7 us (31%)
  waiting for transfers between devices  19.4 us (7%)
  other arithmetic  14.3 us (5%)
  local copies, waits for them, and re-layouts  10.6 us (4%)
    pallas_call x14, Pallas kernels, call(): pl.pallas_call(kernel, grid=grid, in_specs=in_specs, out_specs=out_specs,...  132 us
    all_to_all x3, starting transfers between devices, exchange(): lax.all_to_all(flat, ('grp', 'sub'), split_axis=0, concat_axis=0, tiled=T...  30.5 us
    all_to_all x3, starting transfers between devices, coarse(): back = lax.all_to_all(out, 'sub', split_axis=0, concat_axis=0, tiled=True)  26.3 us
    sub x1, other arithmetic, local(): return (s2 + alpha * d2, r2 - alpha * w2)  11.7 us
    ppermute x6, waiting for transfers between devices, shifted(): return lax.ppermute(x, axis, [(i, (i + by) % count) for i in range(count)])  11.3 us
    all_to_all x1, starting transfers between devices, local(): lax.all_to_all(every, ('grp', 'sub'), split_axis=0, concat_axis=0, tiled=...  9.19 us
    unnamed x37, local copies, waits for them, and re-layouts  7.75 us
    ppermute x2, starting transfers between devices, over_grp(): lax.ppermute(sums, 'grp', [(i, ng - 1 - i) for i in range(ng)])  5.99 us
  transfers between devices with their start and end apart: 17, of which 6 were waited for; matrix products, arithmetic and copies ran while one was open for 1% of the time, Pallas kernels for 42%

profile of v1, /device:TPU:1, one launch (start us, length us, event | category | flops | bytes accessed | tf_op | source)
XLA Modules:
  0.0 258.5 jit_solution(14740282546171132090)
XLA Ops:
  0.6 5.1 %first_rhs.1 = (f32[4,32,8,256]{3,2,1,0:T(8,128)}, s32[32]{0:T(128)}) custom-call(s32[32]{0:T(128)} %pick.1, f32[32,256,128]{2,1,0:T(8,128)} %refs_4_.3, f32[32,8,128]{2,1,0:T(8,128)} %p_ref.11), custom_call_target="tpu_custom_call" | custom-call | flops 67108864 | bytes 5374208 | tf_op jit(solution)/shard_map/first_rhs/pallas_call | solution.py:88
  5.7 0.0 copy-start.10
  5.8 11.5 %all-to-all-start = ((f32[128,8,256]{2,1,0:T(8,128)}), f32[128,8,256]{2,1,0:T(8,128)S(1)}, u32[]{:S(2)}, u32[]{:S(2)}) async-start(f32[128,8,256]{2,1,0:T(8,128)} %bitcast.27), calls=%async_computation | async-start | bytes 2097152 | tf_op jit(solution)/shard_map/all_to_all | solution.py:619
  17.3 3.4 %fine_sent.1 = f32[4,272,128]{2,1,0:T(8,128)} custom-call(s32[4]{0:T(128)} %refs_0_.3, s32[32]{0:T(128)} %get-tuple-element.29.inv, f32[32,256,128]{2,1,0:T(8,128)} %refs_4_.3, f32[32,128,128]{2,1,0:T(8,128)} %fac_ref.5, f32[32,8,128]{2,1,0:T(8,128)} %p_ref.11), custom_call_target="tpu_custom_call" | custom-call | flops 268435456 | bytes 6979728 | tf_op jit(solution)/shard_map/fine_sent/pallas_call | solution.py:88
  20.6 1.7 collective-permute-start
  22.3 0.1 copy.16
  22.4 0.7 reshape.54.nbr
  23.1 11.3 %collective-permute-done.lo_ref = f32[4,272,128]{2,1,0:T(8,128)S(1)} collective-permute-done((f32[4,272,128]{2,1,0:T(8,128)}, f32[4,272,128]{2,1,0:T(8,128)S(1)}, u32[]{:S(2)}, u32[]{:S(2)}) %collective-permute-start) | collective-permute-done | bytes 557088 | tf_op jit(solution)/shard_map/ppermute | solution.py:593
  34.4 0.2 fusion.4
  34.6 2.1 all-to-all-done
  36.7 1.0 copy-done.5
  37.6 4.5 %coarse_solve.3 = f32[32,7,8,128]{3,2,1,0:T(8,128)} custom-call(f32[4,256,256]{2,1,0:T(8,128)} %bitcast.24, f32[1,256,1024]{2,1,0:T(8,128)} %c_ref.5), custom_call_target="tpu_custom_call" | custom-call | flops 402653184 | bytes 3014656 | tf_op jit(solution)/shard_map/coarse_solve/pallas_call | solution.py:88
  42.1 7.4 %all-to-all-start.1 = ((f32[32,7,8,128]{3,2,1,0:T(8,128)}), f32[32,7,8,128]{3,2,1,0:T(8,128)S(1)}, u32[]{:S(2)}, u32[]{:S(2)}) async-start(f32[32,7,8,128]{3,2,1,0:T(8,128)} %coarse_solve.3), calls=%async_computation.1 | async-start | bytes 1835008 | tf_op jit(solution)/shard_map/all_to_all | solution.py:624
  49.5 0.2 fusion.5
  49.7 0.6 pad_add_fusion.cpos
  50.3 0.0 copy-done.13
  50.4 19.7 %fine_operator.3 = (bf16[32,256,256]{2,1,0:T(8,128)(2,1)}, f32[32,256,128]{2,1,0:T(8,128)}, f32[32,8,256]{2,1,0:T(8,128)}, bf16[32,128,128]{2,1,0:T(8,128)(2,1)}, f32[32,8,128]{2,1,0:T(8,128)}) custom-call(s32[128]{0:T(128)} %reshape.54.nbr, f32[32,256,128]{2,1,0:T(8,128)} %refs_4_.3, f32[32,128,128]{2,1,0:T(8,128)} %fac_ref.5, f32[4,272,128]{2,1,0:T(8,128)} %copy-done.12, ...), custom_call_target="tpu_custom_call" | custom-call | flops 7516192768 | bytes 27853312 | tf_op jit(solution)/shard_map/fine_operator/pallas_call | solution.py:88
  70.0 0.0 all-to-all-done.1
  70.1 0.9 copy-done
  71.0 3.8 %next_rhs.2 = (f32[32,8,256]{2,1,0:T(8,128)}, f32[4,32,8,256]{3,2,1,0:T(8,128)}) custom-call(s32[40]{0:T(128)} %pad_add_fusion.cpos, s32[128]{0:T(128)} %reshape.54.nbr, f32[224,8,128]{2,1,0:T(8,128)} %bitcast.14, f32[32,8,256]{2,1,0:T(8,128)} %get-tuple-element.31.paf_ref, f32[32,8,128]{2,1,0:T(8,128)} %get-tuple-element.32.h_ref), custom_call_target="tpu_custom_call" | custom-call | flops 33554432 | bytes 2622112 | tf_op jit(solution)/shard_map/next_rhs/pallas_call | solution.py:88
  74.8 9.9 %all-to-all-start.2 = ((f32[128,8,256]{2,1,0:T(8,128)}), f32[128,8,256]{2,1,0:T(8,128)S(1)}, u32[]{:S(2)}, u32[]{:S(2)}) async-start(f32[128,8,256]{2,1,0:T(8,128)} %bitcast.26), calls=%async_computation.2 | async-start | bytes 2097152 | tf_op jit(solution)/shard_map/all_to_all | solution.py:619
  84.7 10.1 %image.3 = (f32[32,256,128]{2,1,0:T(8,128)}, f32[8,128]{1,0:T(8,128)}, f32[4,256,128]{2,1,0:T(8,128)}) custom-call(s32[40]{0:T(128)} %pad_add_fusion.cpos, s32[128]{0:T(128)} %reshape.54.nbr, s32[4]{0:T(128)} %refs_0_.3, f32[224,8,128]{2,1,0:T(8,128)} %bitcast.15, bf16[32,128,128]{2,1,0:T(8,128)(2,1)} %get-tuple-element.34.refs_2_.refs_1_, ...), custom_call_target="tpu_custom_call" | custom-call | flops 268435456 | bytes 17175216 | tf_op jit(solution)/shard_map/image/pallas_call | solution.py:88
  94.9 1.7 collective-permute-start.4
  96.6 0.0 collective-permute-start.5
  96.6 1.3 collective-permute-start.2
  97.9 1.7 collective-permute-done.2
  99.5 0.7 add.25.refs_0_
  100.2 3.1 %collective-permute-start.3 = (f32[8,128]{1,0:T(8,128)S(1)}, f32[8,128]{1,0:T(8,128)S(1)}, u32[]{:S(2)}, u32[]{:S(2)}) collective-permute-start(f32[8,128]{1,0:T(8,128)S(1)} %add.25.refs_0_), channel_id=1, source_target_pairs={{0,3},{1,2},{2,1},{3,0},{4,7},{5,6},{6,5},{7,4},{8,11},{9,10},{10,... | collective-permute-start | bytes 12296 | tf_op jit(solution)/shard_map/ppermute | solution.py:629
  103.3 1.3 collective-permute-done.3.refs_1_
  104.6 0.6 copy-done.8
  105.2 0.4 copy-done.4
  105.6 4.5 %coarse_solve.4 = f32[32,7,8,128]{3,2,1,0:T(8,128)} custom-call(f32[4,256,256]{2,1,0:T(8,128)} %bitcast.23, f32[1,256,1024]{2,1,0:T(8,128)} %c_ref.5, f32[8,128]{1,0:T(8,128)} %copy-done.6, f32[8,128]{1,0:T(8,128)} %copy-done.8), custom_call_target="tpu_custom_call" | custom-call | flops 402653184 | bytes 3022848 | tf_op jit(solution)/shard_map/coarse_solve/pallas_call | solution.py:88
  110.1 9.4 %all-to-all-start.3 = ((f32[32,7,8,128]{3,2,1,0:T(8,128)}), f32[32,7,8,128]{3,2,1,0:T(8,128)S(1)}, u32[]{:S(2)}, u32[]{:S(2)}) async-start(f32[32,7,8,128]{3,2,1,0:T(8,128)} %coarse_solve.4), calls=%async_computation.3 | async-start | bytes 1835008 | tf_op jit(solution)/shard_map/all_to_all | solution.py:624
  119.5 0.0 collective-permute-done.5.up_ref
  119.5 0.8 copy-done.14
  120.3 0.2 copy-done.16
  120.4 18.6 %fine_operator.4 = (bf16[32,256,256]{2,1,0:T(8,128)(2,1)}, f32[32,256,128]{2,1,0:T(8,128)}, f32[32,8,256]{2,1,0:T(8,128)}) custom-call(s32[128]{0:T(128)} %reshape.54.nbr, f32[32,256,128]{2,1,0:T(8,128)} %get-tuple-element.37.v_ref.refs_5_, f32[32,128,128]{2,1,0:T(8,128)} %fac_ref.5, f32[4,256,128]{2,1,0:T(8,128)} %copy-done.14, f32[4,256,128]{2,1,0:T(8,128)} %copy-done.16, ...), custom_call_target="tpu_custom_call" | custom-call | flops 7516192768 | bytes 26608128 | tf_op jit(solution)/shard_map/fine_operator/pallas_call | solution.py:88
  139.1 0.9 copy-done.1
  140.0 4.0 %next_rhs.3 = (f32[32,8,256]{2,1,0:T(8,128)}, f32[4,32,8,256]{3,2,1,0:T(8,128)}) custom-call(s32[40]{0:T(128)} %pad_add_fusion.cpos, s32[128]{0:T(128)} %reshape.54.nbr, f32[224,8,128]{2,1,0:T(8,128)} %bitcast.17, f32[32,8,256]{2,1,0:T(8,128)} %get-tuple-element.39.paf_ref, f32[32,8,128]{2,1,0:T(8,128)} %get-tuple-element.32.h_ref, ...), custom_call_target="tpu_custom_call" | custom-call | flops 33554432 | bytes 2884256 | tf_op jit(solution)/shard_map/next_rhs/pallas_call | solution.py:88
  144.0 9.2 %all-to-all-start.4 = ((f32[128,8,256]{2,1,0:T(8,128)}), f32[128,8,256]{2,1,0:T(8,128)S(1)}, u32[]{:S(2)}, u32[]{:S(2)}) async-start(f32[128,8,256]{2,1,0:T(8,128)} %bitcast.25), calls=%async_computation.4 | async-start | bytes 2097152 | tf_op jit(solution)/shard_map/all_to_all | solution.py:619
  153.2 12.4 %image.4 = (f32[32,256,128]{2,1,0:T(8,128)}, f32[32,256,128]{2,1,0:T(8,128)}, f32[8,128]{1,0:T(8,128)}, f32[4,256,128]{2,1,0:T(8,128)}) custom-call(s32[40]{0:T(128)} %pad_add_fusion.cpos, s32[128]{0:T(128)} %reshape.54.nbr, s32[4]{0:T(128)} %refs_0_.3, f32[224,8,128]{2,1,0:T(8,128)} %bitcast.18, bf16[32,128,128]{2,1,0:T(8,128)(2,1)} %get-tuple-element.34.refs_2_.refs_1_, ...), custom_call_target="tpu_custom_call" | custom-call | flops 268435456 | bytes 25563824 | tf_op jit(solution)/shard_map/image/pallas_call | solution.py:88
  165.6 1.7 collective-permute-start.8
  167.3 0.0 collective-permute-start.9
  167.3 1.3 collective-permute-start.6
  168.6 1.7 collective-permute-done.6
  170.4 0.7 add.26.refs_0_
  171.0 2.9 %collective-permute-start.7 = (f32[8,128]{1,0:T(8,128)S(1)}, f32[8,128]{1,0:T(8,128)S(1)}, u32[]{:S(2)}, u32[]{:S(2)}) collective-permute-start(f32[8,128]{1,0:T(8,128)S(1)} %add.26.refs_0_), channel_id=1, source_target_pairs={{0,3},{1,2},{2,1},{3,0},{4,7},{5,6},{6,5},{7,4},{8,11},{9,10},{10,... | collective-permute-start | bytes 12296 | tf_op jit(solution)/shard_map/ppermute | solution.py:629
  174.0 1.3 collective-permute-done.7.refs_1_
  175.3 0.6 copy-done.9
  175.9 0.4 copy-done.3
  176.3 4.5 %coarse_solve.5 = f32[32,7,8,128]{3,2,1,0:T(8,128)} custom-call(f32[4,256,256]{2,1,0:T(8,128)} %bitcast.22, f32[1,256,1024]{2,1,0:T(8,128)} %c_ref.5, f32[8,128]{1,0:T(8,128)} %copy-done.7, f32[8,128]{1,0:T(8,128)} %copy-done.9), custom_call_target="tpu_custom_call" | custom-call | flops 402653184 | bytes 3022848 | tf_op jit(solution)/shard_map/coarse_solve/pallas_call | solution.py:88
  180.7 9.4 %all-to-all-start.5 = ((f32[32,7,8,128]{3,2,1,0:T(8,128)}), f32[32,7,8,128]{3,2,1,0:T(8,128)S(1)}, u32[]{:S(2)}, u32[]{:S(2)}) async-start(f32[32,7,8,128]{3,2,1,0:T(8,128)} %coarse_solve.5), calls=%async_computation.5 | async-start | bytes 1835008 | tf_op jit(solution)/shard_map/all_to_all | solution.py:624
  190.2 0.8 copy-done.15
  191.0 0.2 copy-done.17
  191.2 17.8 %fine_operator.5 = (bf16[32,256,256]{2,1,0:T(8,128)(2,1)}, f32[32,256,128]{2,1,0:T(8,128)}) custom-call(s32[128]{0:T(128)} %reshape.54.nbr, f32[32,256,128]{2,1,0:T(8,128)} %get-tuple-element.46.v_ref.refs_4_, f32[32,128,128]{2,1,0:T(8,128)} %fac_ref.5, f32[4,256,128]{2,1,0:T(8,128)} %copy-done.15, f32[4,256,128]{2,1,0:T(8,128)} %copy-done.17, ...), custom_call_target="tpu_custom_call" | custom-call | flops 7516192768 | bytes 26345984 | tf_op jit(solution)/shard_map/fine_operator/pallas_call | solution.py:88
  209.0 0.9 copy-done.2
  210.0 11.6 %image.5 = (f32[32,256,128]{2,1,0:T(8,128)}, f32[32,256,128]{2,1,0:T(8,128)}, f32[8,128]{1,0:T(8,128)}) custom-call(s32[40]{0:T(128)} %pad_add_fusion.cpos, s32[128]{0:T(128)} %reshape.54.nbr, f32[224,8,128]{2,1,0:T(8,128)} %bitcast.20, bf16[32,128,128]{2,1,0:T(8,128)(2,1)} %get-tuple-element.34.refs_2_.refs_1_, f32[32,256,128]{2,1,0:T(8,128)} %get-tuple-element.50.refs_2_, ...), custom_call_target="tpu_custom_call" | custom-call | flops 268435456 | bytes 22942368 | tf_op jit(solution)/shard_map/image/pallas_call | solution.py:88
  221.5 0.8 slice_bitcast_fusion.1
  222.3 0.8 copy.17
  223.1 9.2 %all-to-all-start.6 = ((f32[128,2,128]{2,1,0:T(2,128)}), f32[128,2,128]{2,1,0:T(2,128)S(1)}, u32[]{:S(2)}, u32[]{:S(2)}) async-start(f32[128,2,128]{2,1,0:T(2,128)} %copy.17), calls=%async_computation.6 | async-start | bytes 262144 | tf_op jit(solution)/shard_map/all_to_all | solution.py:665
  232.3 12.4 %combine.1 = (f32[32,256,128]{2,1,0:T(8,128)}, f32[32,256,128]{2,1,0:T(8,128)}) custom-call(s32[40]{0:T(128)} %pad_add_fusion.cpos, f32[224,8,128]{2,1,0:T(8,128)} %bitcast.16, f32[224,8,128]{2,1,0:T(8,128)} %bitcast.19, f32[224,8,128]{2,1,0:T(8,128)} %bitcast.21, f32[32,8,128]{2,1,0:T(8,128)} %p_ref.11, bf16[32,256,256]{2,1,0:T(8,128)(2,1)} %get-tuple-element.44.f0_ref, ...), custom_call_target="tpu_custom_call" | custom-call | flops 805306368 | bytes 23855264 | tf_op jit(solution)/shard_map/combine/pallas_call | solution.py:88
  244.7 0.2 slice_reduce_fusion
  244.9 0.6 fusion.6
  246.9 11.7 %multiply_subtract_fusion = (f32[32,256,128]{2,1,0:T(8,128)}, f32[32,256,128]{2,1,0:T(8,128)}) fusion(f32[32,256,128]{2,1,0:T(8,128)} %get-tuple-element.54, f32[32,256,128]{2,1,0:T(8,128)} %get-tuple-element.55, f32[]{:T(128)} %bitcast.11, f32[32,256,128]{2,1,0:T(8,128)} %get-tuple-element.49, f32[32,256,128]{2,1,0:T(8,128)} %get-tuple-element.53), kind=kLoop, calls=%fused_computation | loop fusion | flops 4194304 | bytes 25165828 | tf_op jit(solution)/shard_map/sub | solution.py:669
  (36 shorter events, 0.1 us)
Async XLA Ops:
  5.7 16.6 %copy-start.10 = (s32[32,4]{0,1:T(4,128)S(1)}, s32[32,4]{0,1:T(4,128)}, u32[]{:S(2)}) copy-start(s32[32,4]{0,1:T(4,128)} %param.16) | copy-start | bytes 1540
  5.7 17.4 %copy-start.11 = (s32[32]{0:T(128)S(1)}, s32[32]{0:T(128)}, u32[]{:S(2)}) copy-start(s32[32]{0:T(128)} %get-tuple-element.29.inv) | copy-start | bytes 388
  5.8 30.9 %all-to-all-start = ((f32[128,8,256]{2,1,0:T(8,128)}), f32[128,8,256]{2,1,0:T(8,128)S(1)}, u32[]{:S(2)}, u32[]{:S(2)}) async-start(f32[128,8,256]{2,1,0:T(8,128)} %bitcast.27), calls=%async_computation | async-start | bytes 2097152 | tf_op jit(solution)/shard_map/all_to_all | solution.py:619
  20.6 13.8 %collective-permute-start = (f32[4,272,128]{2,1,0:T(8,128)}, f32[4,272,128]{2,1,0:T(8,128)S(1)}, u32[]{:S(2)}, u32[]{:S(2)}) collective-permute-start(f32[4,272,128]{2,1,0:T(8,128)} %fine_sent.1), channel_id=1, source_target_pairs={{0,4},{4,8},{8,12},{12,16},{16,20},{20,24},{24,28},{28,32},{32,36}... | collective-permute-start | bytes 1671176 | tf_op jit(solution)/shard_map/ppermute | solution.py:593
  22.3 27.2 %collective-permute-start.1 = (f32[4,272,128]{2,1,0:T(8,128)}, f32[4,272,128]{2,1,0:T(8,128)S(1)}, u32[]{:S(2)}, u32[]{:S(2)}) collective-permute-start(f32[4,272,128]{2,1,0:T(8,128)} %fine_sent.1), channel_id=1, source_target_pairs={{0,124},{4,0},{8,4},{12,8},{16,12},{20,16},{24,20},{28,24},{32,28}... | collective-permute-start | bytes 1671176 | tf_op jit(solution)/shard_map/ppermute | solution.py:593
  34.4 15.9 %copy-start.12 = (f32[4,272,128]{2,1,0:T(8,128)}, f32[4,272,128]{2,1,0:T(8,128)S(1)}, u32[]{:S(2)}) copy-start(f32[4,272,128]{2,1,0:T(8,128)S(1)} %collective-permute-done.lo_ref) | copy-start | bytes 1671172
  36.7 1.0 copy-start.5
  42.1 27.9 %all-to-all-start.1 = ((f32[32,7,8,128]{3,2,1,0:T(8,128)}), f32[32,7,8,128]{3,2,1,0:T(8,128)S(1)}, u32[]{:S(2)}, u32[]{:S(2)}) async-start(f32[32,7,8,128]{3,2,1,0:T(8,128)} %coarse_solve.3), calls=%async_computation.1 | async-start | bytes 1835008 | tf_op jit(solution)/shard_map/all_to_all | solution.py:624
  49.5 0.8 copy-start.13
  70.1 1.0 copy-start
  74.8 29.7 %all-to-all-start.2 = ((f32[128,8,256]{2,1,0:T(8,128)}), f32[128,8,256]{2,1,0:T(8,128)S(1)}, u32[]{:S(2)}, u32[]{:S(2)}) async-start(f32[128,8,256]{2,1,0:T(8,128)} %bitcast.26), calls=%async_computation.2 | async-start | bytes 2097152 | tf_op jit(solution)/shard_map/all_to_all | solution.py:619
  94.9 24.6 %collective-permute-start.4 = (f32[4,256,128]{2,1,0:T(8,128)}, f32[4,256,128]{2,1,0:T(8,128)S(1)}, u32[]{:S(2)}, u32[]{:S(2)}) collective-permute-start(f32[4,256,128]{2,1,0:T(8,128)} %get-tuple-element.38), channel_id=1, source_target_pairs={{0,4},{4,8},{8,12},{12,16},{16,20},{20,24},{24,28},{28,32},{32,36}... | collective-permute-start | bytes 1572872 | tf_op jit(solution)/shard_map/ppermute | solution.py:593
  96.6 22.9 %collective-permute-start.5 = (f32[4,256,128]{2,1,0:T(8,128)}, f32[4,256,128]{2,1,0:T(8,128)S(1)}, u32[]{:S(2)}, u32[]{:S(2)}) collective-permute-start(f32[4,256,128]{2,1,0:T(8,128)} %get-tuple-element.38), channel_id=1, source_target_pairs={{0,124},{4,0},{8,4},{12,8},{16,12},{20,16},{24,20},{28,24},{32,28}... | collective-permute-start | bytes 1572872 | tf_op jit(solution)/shard_map/ppermute | solution.py:593
  96.6 3.0 %collective-permute-start.2 = (f32[8,128]{1,0:T(8,128)}, f32[8,128]{1,0:T(8,128)S(1)}, u32[]{:S(2)}, u32[]{:S(2)}) collective-permute-start(f32[8,128]{1,0:T(8,128)} %get-tuple-element.36), channel_id=1, source_target_pairs={{0,1},{1,0},{2,3},{3,2},{4,5},{5,4},{6,7},{7,6},{8,9},{9,8},{10,11... | collective-permute-start | bytes 12296 | tf_op jit(solution)/shard_map/ppermute | solution.py:628
  100.2 4.4 %copy-start.6 = (f32[8,128]{1,0:T(8,128)}, f32[8,128]{1,0:T(8,128)S(1)}, u32[]{:S(2)}) copy-start(f32[8,128]{1,0:T(8,128)S(1)} %add.25.refs_0_) | copy-start | bytes 12292
  100.2 4.3 %collective-permute-start.3 = (f32[8,128]{1,0:T(8,128)S(1)}, f32[8,128]{1,0:T(8,128)S(1)}, u32[]{:S(2)}, u32[]{:S(2)}) collective-permute-start(f32[8,128]{1,0:T(8,128)S(1)} %add.25.refs_0_), channel_id=1, source_target_pairs={{0,3},{1,2},{2,1},{3,0},{4,7},{5,6},{6,5},{7,4},{8,11},{9,10},{10,... | collective-permute-start | bytes 12296 | tf_op jit(solution)/shard_map/ppermute | solution.py:629
  104.6 0.6 copy-start.8
  104.6 1.0 copy-start.4
  110.1 29.0 %all-to-all-start.3 = ((f32[32,7,8,128]{3,2,1,0:T(8,128)}), f32[32,7,8,128]{3,2,1,0:T(8,128)S(1)}, u32[]{:S(2)}, u32[]{:S(2)}) async-start(f32[32,7,8,128]{3,2,1,0:T(8,128)} %coarse_solve.4), calls=%async_computation.3 | async-start | bytes 1835008 | tf_op jit(solution)/shard_map/all_to_all | solution.py:624
  119.5 0.8 copy-start.14
  119.5 0.9 copy-start.16
  139.1 0.9 copy-start.1
  144.0 31.3 %all-to-all-start.4 = ((f32[128,8,256]{2,1,0:T(8,128)}), f32[128,8,256]{2,1,0:T(8,128)S(1)}, u32[]{:S(2)}, u32[]{:S(2)}) async-start(f32[128,8,256]{2,1,0:T(8,128)} %bitcast.25), calls=%async_computation.4 | async-start | bytes 2097152 | tf_op jit(solution)/shard_map/all_to_all | solution.py:619
  165.6 24.6 %collective-permute-start.8 = (f32[4,256,128]{2,1,0:T(8,128)}, f32[4,256,128]{2,1,0:T(8,128)S(1)}, u32[]{:S(2)}, u32[]{:S(2)}) collective-permute-start(f32[4,256,128]{2,1,0:T(8,128)} %get-tuple-element.47), channel_id=1, source_target_pairs={{0,4},{4,8},{8,12},{12,16},{16,20},{20,24},{24,28},{28,32},{32,36}... | collective-permute-start | bytes 1572872 | tf_op jit(solution)/shard_map/ppermute | solution.py:593
  167.3 22.9 %collective-permute-start.9 = (f32[4,256,128]{2,1,0:T(8,128)}, f32[4,256,128]{2,1,0:T(8,128)S(1)}, u32[]{:S(2)}, u32[]{:S(2)}) collective-permute-start(f32[4,256,128]{2,1,0:T(8,128)} %get-tuple-element.47), channel_id=1, source_target_pairs={{0,124},{4,0},{8,4},{12,8},{16,12},{20,16},{24,20},{28,24},{32,28}... | collective-permute-start | bytes 1572872 | tf_op jit(solution)/shard_map/ppermute | solution.py:593
  167.3 3.1 %collective-permute-start.6 = (f32[8,128]{1,0:T(8,128)}, f32[8,128]{1,0:T(8,128)S(1)}, u32[]{:S(2)}, u32[]{:S(2)}) collective-permute-start(f32[8,128]{1,0:T(8,128)} %get-tuple-element.43), channel_id=1, source_target_pairs={{0,1},{1,0},{2,3},{3,2},{4,5},{5,4},{6,7},{7,6},{8,9},{9,8},{10,11... | collective-permute-start | bytes 12296 | tf_op jit(solution)/shard_map/ppermute | solution.py:628
  171.0 4.2 %copy-start.7 = (f32[8,128]{1,0:T(8,128)}, f32[8,128]{1,0:T(8,128)S(1)}, u32[]{:S(2)}) copy-start(f32[8,128]{1,0:T(8,128)S(1)} %add.26.refs_0_) | copy-start | bytes 12292
  171.0 4.2 %collective-permute-start.7 = (f32[8,128]{1,0:T(8,128)S(1)}, f32[8,128]{1,0:T(8,128)S(1)}, u32[]{:S(2)}, u32[]{:S(2)}) collective-permute-start(f32[8,128]{1,0:T(8,128)S(1)} %add.26.refs_0_), channel_id=1, source_target_pairs={{0,3},{1,2},{2,1},{3,0},{4,7},{5,6},{6,5},{7,4},{8,11},{9,10},{10,... | collective-permute-start | bytes 12296 | tf_op jit(solution)/shard_map/ppermute | solution.py:629
  175.3 0.6 copy-start.9
  175.3 1.0 copy-start.3
  180.7 28.3 %all-to-all-start.5 = ((f32[32,7,8,128]{3,2,1,0:T(8,128)}), f32[32,7,8,128]{3,2,1,0:T(8,128)S(1)}, u32[]{:S(2)}, u32[]{:S(2)}) async-start(f32[32,7,8,128]{3,2,1,0:T(8,128)} %coarse_solve.5), calls=%async_computation.5 | async-start | bytes 1835008 | tf_op jit(solution)/shard_map/all_to_all | solution.py:624
  190.2 0.8 copy-start.15
  190.2 1.0 copy-start.17
  209.0 0.9 copy-start.2
  223.1 21.6 %all-to-all-start.6 = ((f32[128,2,128]{2,1,0:T(2,128)}), f32[128,2,128]{2,1,0:T(2,128)S(1)}, u32[]{:S(2)}, u32[]{:S(2)}) async-start(f32[128,2,128]{2,1,0:T(2,128)} %copy.17), calls=%async_computation.6 | async-start | bytes 262144 | tf_op jit(solution)/shard_map/all_to_all | solution.py:665
